TPU v7x, 32 devices: a whole 2x2x4 slice. The times are simulated.
32 devices in a mesh: parts: 2 (over x), node: 8 (over z, y), local: 2 (over core).
Axes of the slice: x: 2, y: 2, z: 4, core: 2. Of those that a mesh axis runs over, the one named last changes fastest.
Arguments:
- attn_partial: bfloat16 [2, 4096, 6144], P('local', ('parts', 'node')), parts along dimension 1, may hold values from -4 to 4
- residual: bfloat16 [4096, 6144], P(('parts', 'node', 'local')), parts along dimension 0, may hold values from -4 to 4
- norm_gain: float32 [6144], replicated, may hold values from 0.5 to 1.5
- expert_ids: int32 [4096, 4], P(('parts', 'node', 'local')), parts along dimension 0, may hold values from 0 to 7, all different within a row; in each aligned block of 128 rows (0 to 127, 128 to 255, ...) at most 96 rows name the same one
- gate_weights: float32 [4096, 4], P(('parts', 'node', 'local')), parts along dimension 0, may hold values from 0.05 to 0.45
- up_weight: bfloat16 [8, 6144, 1536], P('node', None, 'local'), may hold values from -0.078125 to 0.078125
- down_weight: bfloat16 [8, 1536, 6144], P('node', 'local'), may hold values from -0.15625 to 0.15625
Outputs:
- layer_out: bfloat16 [4096, 6144], P(('parts', 'node', 'local')), parts along dimension 0
There are 2 independent parts, one for each index of `parts`. A program takes and returns all parts, laid end to end along the dimension named above; an argument that names none is the same for every part. Nothing has to cross between parts.
Inputs may be any that keep to these rules, and one draw needn't show every extreme that they name: `expert_ids`: each token names 4 different experts. Within each aligned block of 128 tokens (the tokens of one device) no expert is named by more than 96 tokens, and in every draw some expert is named by exactly 96 tokens of some block.
All inputs are finite; a program needn't handle non-finite values.
Results may differ from a plain program's by a relative error of at most 0.0095.
Values may be sent and summed in bfloat16 or wider, within the bound.
A program may use at most 192 MiB of HBM per device.

v0:
```python
import jax
import jax.numpy as jnp
from jax import lax
from jax.sharding import PartitionSpec as P


def on_device(attn_partial, residual, norm_gain, expert_ids, gate_weights, up_weight, down_weight):
    attention = lax.psum_scatter(attn_partial, "local", scatter_dimension=1, tiled=True).astype(
        jnp.float32
    )[0]
    hidden_state = residual.astype(jnp.float32) + attention
    mean_square = jnp.mean(hidden_state * hidden_state, axis=-1, keepdims=True)
    normed = (hidden_state * lax.rsqrt(mean_square + 1e-06) * norm_gain).astype(jnp.bfloat16)
    token_count = residual.shape[0]
    width = residual.shape[1]
    top_count = expert_ids.shape[1]
    expert_count = lax.axis_size("node")
    local_count = lax.axis_size("local")
    capacity = token_count * top_count * 3 // (2 * expert_count)
    flat_ids = expert_ids.reshape(-1)
    expert_hot = (flat_ids[:, None] == jnp.arange(expert_count, dtype=jnp.int32)[None, :]).astype(
        jnp.int32
    )
    slot_rank = jnp.sum((jnp.cumsum(expert_hot, axis=0) - expert_hot) * expert_hot, axis=1)
    slot_index = flat_ids * capacity + slot_rank
    repeated = jnp.repeat(normed, top_count, axis=0)
    send_rows = (
        jnp.zeros((expert_count * capacity, width), jnp.bfloat16).at[slot_index].set(repeated)
    )
    duplicated = jnp.broadcast_to(
        send_rows.reshape(expert_count, 1, capacity, width),
        (expert_count, local_count, capacity, width),
    )
    duplicated = duplicated.reshape(expert_count * local_count, capacity, width)
    arrived = lax.all_to_all(duplicated, ("node", "local"), split_axis=0, concat_axis=0, tiled=True)
    arrived = arrived.reshape(expert_count, local_count, capacity, width)
    recv_rows = arrived.reshape(-1, width)
    activated = jax.nn.silu(
        jnp.dot(recv_rows, up_weight[0], preferred_element_type=jnp.float32)
    ).astype(jnp.bfloat16)
    partial_out = jnp.dot(activated, down_weight[0], preferred_element_type=jnp.float32).astype(
        jnp.bfloat16
    )
    partial_out = partial_out.reshape(expert_count, local_count, capacity, width)
    summed_rows = lax.psum_scatter(partial_out, "local", scatter_dimension=1, tiled=True).astype(
        jnp.float32
    )
    returned = lax.all_to_all(
        summed_rows.astype(jnp.bfloat16), "node", split_axis=0, concat_axis=0, tiled=True
    )
    result_rows = returned.reshape(expert_count * capacity, width)
    chosen = result_rows[slot_index].reshape(token_count, top_count, width)
    combined = jnp.sum(gate_weights[:, :, None] * chosen.astype(jnp.float32), axis=1)
    return (hidden_state + combined).astype(jnp.bfloat16)


def solution(mesh):
    in_specs = (
        P("local", ("parts", "node"), None),
        P(("parts", "node", "local"), None),
        P(),
        P(("parts", "node", "local"), None),
        P(("parts", "node", "local"), None),
        P("node", None, "local"),
        P("node", "local", None),
    )
    out_specs = P(("parts", "node", "local"), None)
    return jax.shard_map(
        on_device, mesh=mesh, in_specs=in_specs, out_specs=out_specs, check_vma=False
    )
```

profile of v0, /device:TPU:0, one launch (start us, length us, event | category | flops | bytes accessed | tf_op | source)
XLA Modules:
  0.0 857.0 jit_solution(8626851622188831756)
XLA Ops:
  6.5 0.0 copy-start
  6.5 0.0 copy-start.2
  6.5 0.0 reduce-scatter.5.cloned.1.call-start
  6.5 0.7 reduce-scatter.5.cloned.1.call-update
  7.3 0.0 all-reduce.3.cloned.1.call-start
  7.3 0.8 copy.15
  8.1 0.1 eq.29
  8.2 0.1 eq.25
  8.3 1.1 reduce-window.6
  9.5 0.2 slice_reduce_fusion
  9.7 0.7 broadcast_multiply_fusion
  10.4 0.1 copy.14
  10.5 0.1 mul.53
  10.6 0.1 fusion.8
  10.7 12.5 %reduce-scatter.5.cloned.1.call-done = bf16[1,128,6144]{2,1,0:T(8,128)(2,1)} async-done(((bf16[1,256,6144]{2,1,0:T(8,128)(2,1)}), bf16[1,128,6144]{2,1,0:T(8,128)(2,1)}) %reduce-scatter.5.cloned.1.call-update) | async-done | bytes 1572880 | tf_op jit(solution)/shard_map/reduce_scatter | solution.py:8
  23.2 2.5 multiply_reduce_fusion.1
  25.7 0.0 copy-done
  25.7 0.0 copy-done.2
  25.8 2.0 multiply_convert_fusion.1
  27.8 5.2 broadcast_in_dim.9
  33.0 10.4 %reshape.92 = bf16[512,6144]{1,0:T(8,128)(2,1)} reshape(bf16[128,4,6144]{2,1,0:T(4,128)(2,1)} %broadcast_in_dim.9) | data formatting | bytes 12582912 | tf_op jit(solution)/shard_map/reshape | solution.py:26
  43.4 16.3 %scatter_custom_fusion = bf16[768,6144]{1,0:T(8,128)(2,1)} fusion(s32[512]{0:T(512)S(1)} %bitcast.41, bf16[512,6144]{1,0:T(8,128)(2,1)} %reshape.92, bf16[]{:T(256)} %constant.8.clone.1), kind=kCustom, calls=%fused_computation.8 | custom fusion | bytes 9437696 | tf_op jit(solution)/shard_map/scatter | solution.py:28
  59.7 8.0 broadcast_in_dim.22
  67.7 412.5 %all_to_all.10 = bf16[16,96,6144]{2,1,0:T(8,128)(2,1)S(1)} all-to-all(bf16[16,96,6144]{2,1,0:T(8,128)(2,1)S(1)} %bitcast.37), channel_id=1, replica_groups=mesh['parts'=2,'node'=8,'local'=2] {'node','local'}, dimensions={0} | all-to-all | bytes 37748736 | tf_op jit(solution)/shard_map/all_to_all | solution.py:35
  480.2 19.0 %multiply_convert_fusion = bf16[1536,768]{1,0:T(8,128)(2,1)S(1)} fusion(bf16[1536,6144]{1,0:T(8,128)(2,1)S(1)} %bitcast.40, bf16[1,6144,768]{2,1,0:T(8,128)(2,1)} %param.12), kind=kOutput, calls=%fused_computation.7 | convolution fusion | flops 14501412864 | bytes 30670848 | tf_op jit(solution)/shard_map/dot_general | solution.py:39
  499.2 21.8 %convolution_convert_fusion = bf16[1536,6144]{1,0:T(8,128)(2,1)} fusion(bf16[1536,768]{1,0:T(8,128)(2,1)S(1)} %multiply_convert_fusion, bf16[1,768,6144]{2,1,0:T(8,128)(2,1)} %param.13), kind=kOutput, calls=%fused_computation.2 | convolution fusion | flops 14504951808 | bytes 30670848 | tf_op jit(solution)/shard_map/dot_general | solution.py:41
  521.0 0.0 copy-start.4
  521.0 0.0 all-reduce.3.cloned.1.call-update
  521.0 0.6 copy-done.4
  521.6 0.6 dynamic-slice
  522.2 64.6 %all-reduce.3.cloned.1.call-done = bf16[8,2,96,6144]{3,2,1,0:T(8,128)(2,1)} async-done(((bf16[8,2,96,6144]{3,2,1,0:T(8,128)(2,1)}), bf16[8,2,96,6144]{3,2,1,0:T(8,128)(2,1)}) %all-reduce.3.cloned.1.call-update) | async-done | bytes 18874384
  586.8 9.2 %constant_dynamic-slice_fusion = bf16[8,1,96,6144]{3,2,1,0:T(8,128)(2,1)} fusion(bf16[8,2,96,6144]{3,2,1,0:T(8,128)(2,1)} %all-reduce.3.cloned.1.call-done, u32[]{:T(128)} %bitcast.20), kind=kLoop, calls=%fused_computation.24 | loop fusion | bytes 18874372
  596.1 0.0 copy-start.3
  596.1 6.0 all-to-all-start.1
  602.1 0.0 copy-done.3
  602.1 0.1 copy.13
  602.2 206.0 %all-to-all-done.1 = bf16[8,1,96,6144]{3,2,1,0:T(8,128)(2,1)} async-done(((bf16[8,1,96,6144]{3,2,1,0:T(8,128)(2,1)}), bf16[8,1,96,6144]{3,2,1,0:T(8,128)(2,1)}, u32[]{:S(2)}, u32[]{:S(2)}) %all-to-all-start.1) | async-done | bytes 9437216 | tf_op jit(solution)/shard_map/all_to_all | solution.py:48
  808.2 17.1 %gather_fusion = bf16[512,6144]{1,0:T(8,128)(2,1)} fusion(bf16[768,6144]{1,0:T(8,128)(2,1)} %bitcast.11, s32[1024]{0:T(1024)S(1)} %pad_clamp_fusion), kind=kCustom, calls=%fused_computation | custom fusion | bytes 12584960 | tf_op jit(solution)/shard_map/gather | solution.py:52
  825.2 12.0 %reshape.79 = f32[128,4,6144]{2,1,0:T(4,128)} reshape(bf16[512,6144]{1,0:T(8,128)(2,1)} %gather_fusion) | data formatting | bytes 18874368 | tf_op jit(solution)/shard_map/convert_element_type | solution.py:53
  837.2 0.0 copy-start.1
  837.2 11.3 %multiply_reduce_fusion = f32[128,6144]{1,0:T(8,128)S(1)} fusion(f32[128,4,6144]{2,1,0:T(4,128)} %reshape.79, f32[128,4]{1,0:T(8,128)S(1)} %copy.13), kind=kLoop, calls=%fused_computation.3 | loop fusion | flops 5505024 | bytes 15730688 | tf_op jit(solution)/shard_map/reduce_sum | solution.py:53
  848.5 0.0 copy-done.1
  848.5 1.7 add_convert_fusion
  (6 shorter events, 0.1 us)
Async XLA Ops:
  6.5 19.2 %copy-start = (bf16[128,6144]{1,0:T(8,128)(2,1)S(1)}, bf16[128,6144]{1,0:T(8,128)(2,1)}, u32[]{:S(2)}) copy-start(bf16[128,6144]{1,0:T(8,128)(2,1)} %param.8) | copy-start | bytes 4718596
  6.5 19.2 %copy-start.2 = (f32[6144]{0:T(1024)S(1)}, f32[6144]{0:T(1024)}, u32[]{:S(2)}) copy-start(f32[6144]{0:T(1024)} %param.9) | copy-start | bytes 73732
  6.5 16.7 %reduce-scatter.5.cloned.1.call-start = ((), (), s32[]{:S(2)}) async-start(), calls=%async_computation.3 | async-start | bytes 4718592 | tf_op jit(solution)/shard_map/reduce_scatter | solution.py:8
  7.3 579.6 %all-reduce.3.cloned.1.call-start = ((), (), s32[]{:S(2)}) async-start(), calls=%async_computation.4 | async-start | bytes 37748736
  521.0 0.7 copy-start.4
  596.1 6.0 copy-start.3
  596.1 212.1 %all-to-all-start.1 = ((bf16[8,1,96,6144]{3,2,1,0:T(8,128)(2,1)}), bf16[8,1,96,6144]{3,2,1,0:T(8,128)(2,1)}, u32[]{:S(2)}, u32[]{:S(2)}) async-start(bf16[8,1,96,6144]{3,2,1,0:T(8,128)(2,1)} %constant_dynamic-slice_fusion), calls=%async_computation.2 | async-start | bytes 18874368 | tf_op jit(solution)/shard_map/all_to_all | solution.py:48
  837.2 11.3 %copy-start.1 = (bf16[1,128,6144]{2,1,0:T(8,128)(2,1)S(1)}, bf16[1,128,6144]{2,1,0:T(8,128)(2,1)}, u32[]{:S(2)}) copy-start(bf16[1,128,6144]{2,1,0:T(8,128)(2,1)} %reduce-scatter.5.cloned.1.call-done) | copy-start | bytes 4718596
Sparse Core Ops, SparseCore 0:
  9.6 13.6 reduce-scatter.4
  521.1 65.6 all-reduce.2
where the time goes:
time: 858 us; the launch traced here: 857 us
  blocking collectives  413 us (48%)
  waiting for transfers between devices  284 us (33%)
  local copies, waits for them, and re-layouts  81 us (9%)
  matrix products  40.8 us (5%)
  other arithmetic  19.4 us (2%)
  between operations  13.5 us (2%)
    all_to_all x1, blocking collectives, on_device(): lax.all_to_all(duplicated, ('node', 'local'), split_axis=0, concat_axis=0...  413 us
    all_to_all x1, waiting for transfers between devices, on_device(): lax.all_to_all(summed_rows.astype(jnp.bfloat16), 'node', split_axis=0, co...  206 us
    unnamed x3, waiting for transfers between devices  65.4 us
    dot_general x1, matrix products, on_device(): jnp.dot(activated, down_weight[0], preferred_element_type=jnp.float32)  21.8 us
    dot_general x1, matrix products, on_device(): jnp.dot(recv_rows, up_weight[0], preferred_element_type=jnp.float32)  19 us
  transfers between devices with their start and end apart: 3, of which 3 were waited for; matrix products, arithmetic and copies ran while one was open for 0% of the time, Pallas kernels for 0%

commit v1 on v0

v1 whole, which is shorter than its diff:
```python
import jax
import jax.numpy as jnp
from jax import lax
from jax.sharding import PartitionSpec as P


def on_device(attn_partial, residual, norm_gain, expert_ids, gate_weights, up_weight, down_weight):
    up = lax.all_gather(up_weight[0], "local", axis=0)
    down = lax.all_gather(down_weight[0], "local", axis=0)
    attention = lax.psum_scatter(attn_partial, "local", scatter_dimension=1, tiled=True).astype(
        jnp.float32
    )[0]
    hidden_state = residual.astype(jnp.float32) + attention
    mean_square = jnp.mean(hidden_state * hidden_state, axis=-1, keepdims=True)
    normed = (hidden_state * lax.rsqrt(mean_square + 1e-06) * norm_gain).astype(jnp.bfloat16)
    expert_count = lax.axis_size("node")
    experts = jnp.arange(expert_count, dtype=jnp.int32)
    dense_gates = jnp.sum(
        jnp.where(expert_ids[:, :, None] == experts, gate_weights[:, :, None], 0.0), axis=1
    )
    gates = lax.all_gather(dense_gates, "node", axis=0, tiled=True)
    me = lax.axis_index("node")
    gate = jnp.sum(jnp.where(experts == me, gates, 0.0), axis=1, keepdims=True)
    rows = lax.all_gather(normed, "node", axis=0, tiled=True)
    total = 0.0
    for half in range(up.shape[0]):
        activated = jax.nn.silu(
            jnp.dot(rows, up[half], preferred_element_type=jnp.float32)
        ).astype(jnp.bfloat16)
        total = total + jnp.dot(activated, down[half], preferred_element_type=jnp.float32)
    weighted = (gate * total).astype(jnp.bfloat16)
    combined = lax.psum_scatter(weighted, "node", scatter_dimension=0, tiled=True)
    return (hidden_state + combined.astype(jnp.float32)).astype(jnp.bfloat16)


def solution(mesh):
    in_specs = (
        P("local", ("parts", "node"), None),
        P(("parts", "node", "local"), None),
        P(),
        P(("parts", "node", "local"), None),
        P(("parts", "node", "local"), None),
        P("node", None, "local"),
        P("node", "local", None),
    )
    out_specs = P(("parts", "node", "local"), None)
    return jax.shard_map(
        on_device, mesh=mesh, in_specs=in_specs, out_specs=out_specs, check_vma=False
    )
```

time: 858 us -> 531 us (0.62)
  blocking collectives: 413 us -> 30.7 us
  waiting for transfers between devices: 284 us -> 410 us
  local copies, waits for them, and re-layouts: 81 us -> 0.07 us
  matrix products: 40.8 us -> 69 us
  other arithmetic: 19.4 us -> 7.21 us
    all_to_all x1 -> x0, blocking collectives: 413 us -> none  [on_device(): lax.all_to_all(duplicated, ('node', 'local'), split_axis=0, concat_axis=0...]
    reduce_scatter x0 -> x1, waiting for transfers between devices: none -> 209 us  [on_device(): lax.psum_scatter(weighted, 'node', scatter_dimension=0, tiled=True)]
    all_to_all x1 -> x0, waiting for transfers between devices: 206 us -> none  [on_device(): lax.all_to_all(summed_rows.astype(jnp.bfloat16), 'node', split_axis=0, co...]
    all_gather x0 -> x3, waiting for transfers between devices: none -> 184 us  [the longest x1 180 us: on_device(): rows = lax.all_gather(normed, 'node', axis=0, tiled=True)]
    unnamed x3 -> x5, waiting for transfers between devices: 65.4 us -> 1.96 us
    all_gather x0 -> x1, blocking collectives: none -> 30.7 us  [on_device(): gates = lax.all_gather(dense_gates, 'node', axis=0, tiled=True)]
    dot_general x2 -> x4, matrix products: 40.8 us -> 69 us  [the longest x2 38.5 us: on_device(): jnp.dot(activated, down[half], preferred_element_type=jnp.float32)]
    gather x1 -> x0, local copies, waits for them, and re-layouts: 17.1 us -> none  [on_device(): chosen = result_rows[slot_index].reshape(token_count, top_count, width)]
  transfers between devices with their start and end apart: 3 -> 5, of which waited for: 3 -> 5; matrix products, arithmetic and copies ran while one was open for 0% -> 6% of each run, Pallas kernels for 0% -> 0%
where the time goes in v1:
time: 531 us; the launch traced here: 530 us
  waiting for transfers between devices  410 us (77%)
  matrix products  69 us (13%)
  blocking collectives  30.7 us (6%)
  between operations  13.2 us (2%)
  other arithmetic  7.21 us (1%)
    reduce_scatter x1, waiting for transfers between devices, on_device(): lax.psum_scatter(weighted, 'node', scatter_dimension=0, tiled=True)  209 us
    all_gather x1, waiting for transfers between devices, on_device(): rows = lax.all_gather(normed, 'node', axis=0, tiled=True)  180 us
    dot_general x2, matrix products, on_device(): jnp.dot(activated, down[half], preferred_element_type=jnp.float32)  38.5 us
    all_gather x1, blocking collectives, on_device(): gates = lax.all_gather(dense_gates, 'node', axis=0, tiled=True)  30.7 us
    dot_general x2, matrix products, on_device(): jnp.dot(rows, up[half], preferred_element_type=jnp.float32)  30.5 us
    reduce_scatter x1, waiting for transfers between devices, on_device(): lax.psum_scatter(attn_partial, 'local', scatter_dimension=1, tiled=True)  15.2 us
  transfers between devices with their start and end apart: 5, of which 5 were waited for; matrix products, arithmetic and copies ran while one was open for 6% of the time, Pallas kernels for 0%

profile of v1, /device:TPU:0, one launch (start us, length us, event | category | flops | bytes accessed | tf_op | source)
XLA Modules:
  0.0 530.5 jit_solution(4680628488906053466)
XLA Ops:
  6.5 0.0 reduce-scatter.3.cloned.1.call-start
  6.5 0.7 reduce-scatter.3.cloned.1.call-update
  7.3 0.0 copy-start
  7.3 0.0 all-gather.6.cloned.1.call-start
  7.3 0.7 all-gather.6.cloned.1.call-update
  8.0 0.0 copy-start.2
  8.0 0.0 all-gather.4.cloned.1.call-start
  8.1 15.2 %reduce-scatter.3.cloned.1.call-done = bf16[1,128,6144]{2,1,0:T(8,128)(2,1)} async-done(((bf16[1,256,6144]{2,1,0:T(8,128)(2,1)}), bf16[1,128,6144]{2,1,0:T(8,128)(2,1)}) %reduce-scatter.3.cloned.1.call-update) | async-done | bytes 1572880 | tf_op jit(solution)/shard_map/reduce_scatter | solution.py:10
  23.2 0.0 copy-done
  23.2 0.0 copy-start.1
  23.3 2.1 multiply_reduce_fusion
  25.4 0.0 copy-done.2
  25.4 0.0 copy-done.1
  25.4 1.7 multiply_convert_fusion.3
  27.1 0.0 all-gather.4.cloned.1.call-update
  27.1 0.0 copy-start.3
  27.2 0.0 copy-start.4
  27.2 0.0 all-gather.8.cloned.1.call-start
  27.2 0.5 all-gather.8.cloned.1.call-update
  27.8 0.0 reduce-scatter.5.cloned.1.call-start
  27.8 0.0 copy-done.3
  27.8 0.0 copy-done.4
  27.9 30.7 %all_gather.12 = f32[1024,8]{0,1:T(8,128)S(1)} all-gather(f32[128,8]{0,1:T(8,128)S(1)} %select_reduce_fusion.1), channel_id=1, replica_groups=mesh['parts'=2,'node'=8,'local'=2] {'node'}, dimensions={0}, use_global_device_ids=true | all-gather | bytes 36864 | tf_op jit(solution)/shard_map/all_gather | solution.py:21
  58.6 0.1 select_reduce_fusion
  58.7 1.2 all-gather.6.cloned.1.call-done
  59.9 180.1 %all-gather.4.cloned.1.call-done = bf16[1024,6144]{1,0:T(8,128)(2,1)} async-done(((bf16[128,6144]{1,0:T(8,128)(2,1)}), bf16[1024,6144]{1,0:T(8,128)(2,1)}) %all-gather.4.cloned.1.call-update) | async-done | bytes 12582928 | tf_op jit(solution)/shard_map/all_gather | solution.py:24
  240.0 0.0 copy-start.5
  240.0 17.0 %multiply_convert_fusion.1 = bf16[1024,768]{1,0:T(8,128)(2,1)} fusion(bf16[1024,6144]{1,0:T(8,128)(2,1)} %all-gather.4.cloned.1.call-done, bf16[2,6144,768]{2,1,0:T(8,128)(2,1)} %all-gather.6.cloned.1.call-done), kind=kOutput, calls=%fused_computation.10 | convolution fusion | flops 9667608576 | bytes 23592960 | tf_op jit(solution)/shard_map/dot_general | solution.py:28
  257.0 0.0 copy-done.5
  257.0 13.5 %multiply_convert_fusion.2 = bf16[1024,768]{1,0:T(8,128)(2,1)} fusion(bf16[1024,6144]{1,0:T(8,128)(2,1)S(1)} %copy-done.5, bf16[2,6144,768]{2,1,0:T(8,128)(2,1)} %all-gather.6.cloned.1.call-done), kind=kOutput, calls=%fused_computation.11 | convolution fusion | flops 9667608576 | bytes 23592960 | tf_op jit(solution)/shard_map/dot_general | solution.py:28
  270.5 3.0 all-gather.8.cloned.1.call-done
  273.5 0.0 copy-start.6
  273.5 17.7 %fusion.1 = f32[1024,6144]{1,0:T(8,128)} fusion(bf16[1024,768]{1,0:T(8,128)(2,1)} %multiply_convert_fusion.2, bf16[2,768,6144]{2,1,0:T(8,128)(2,1)} %all-gather.8.cloned.1.call-done), kind=kOutput, calls=%fused_computation.5 | convolution fusion | flops 9663676416 | bytes 36175872 | tf_op jit(solution)/shard_map/dot_general | solution.py:30
  291.2 0.0 copy-done.6
  291.2 20.8 %multiply_convert_fusion = bf16[1024,6144]{1,0:T(8,128)(2,1)} fusion(f32[1024,6144]{1,0:T(8,128)} %fusion.1, bf16[1024,768]{1,0:T(8,128)(2,1)S(1)} %copy-done.6, f32[1024]{0:T(1024)S(1)} %select_reduce_fusion, bf16[2,768,6144]{2,1,0:T(8,128)(2,1)} %all-gather.8.cloned.1.call-done), kind=kOutput, calls=%fused_computation | convolution fusion | flops 9682550784 | bytes 48762880 | tf_op jit(solution)/shard_map/dot_general | solution.py:30
  312.0 0.0 reduce-scatter.5.cloned.1.call-update
  312.0 208.7 %reduce-scatter.5.cloned.1.call-done = bf16[128,6144]{1,0:T(8,128)(2,1)} async-done(((bf16[1024,6144]{1,0:T(8,128)(2,1)}), bf16[128,6144]{1,0:T(8,128)(2,1)}) %reduce-scatter.5.cloned.1.call-update) | async-done | bytes 1572880 | tf_op jit(solution)/shard_map/reduce_scatter | solution.py:32
  520.7 3.3 add_convert_fusion
  (3 shorter events, 0.0 us)
Async XLA Ops:
  6.5 16.7 %reduce-scatter.3.cloned.1.call-start = ((), (), s32[]{:S(2)}) async-start(), calls=%async_computation.2 | async-start | bytes 4718592 | tf_op jit(solution)/shard_map/reduce_scatter | solution.py:10
  7.3 16.0 %copy-start = (bf16[128,6144]{1,0:T(8,128)(2,1)S(1)}, bf16[128,6144]{1,0:T(8,128)(2,1)}, u32[]{:S(2)}) copy-start(bf16[128,6144]{1,0:T(8,128)(2,1)} %param.8) | copy-start | bytes 4718596
  7.3 52.6 %all-gather.6.cloned.1.call-start = ((), (), s32[]{:S(2)}) async-start(), calls=%async_computation.4 | async-start | bytes 28311552 | tf_op jit(solution)/shard_map/all_gather | solution.py:8
  8.0 17.4 %copy-start.2 = (f32[6144]{0:T(1024)S(1)}, f32[6144]{0:T(1024)}, u32[]{:S(2)}) copy-start(f32[6144]{0:T(1024)} %param.9) | copy-start | bytes 73732
  8.0 231.9 %all-gather.4.cloned.1.call-start = ((), (), s32[]{:S(2)}) async-start(), calls=%async_computation.3 | async-start | bytes 14155776 | tf_op jit(solution)/shard_map/all_gather | solution.py:24
  23.2 2.1 copy-start.1
  27.1 0.7 copy-start.3
  27.2 0.7 copy-start.4
  27.2 246.3 %all-gather.8.cloned.1.call-start = ((), (), s32[]{:S(2)}) async-start(), calls=%async_computation.5 | async-start | bytes 28311552 | tf_op jit(solution)/shard_map/all_gather | solution.py:9
  27.8 493.0 %reduce-scatter.5.cloned.1.call-start = ((), (), s32[]{:S(2)}) async-start(), calls=%async_computation.6 | async-start | bytes 14155776 | tf_op jit(solution)/shard_map/reduce_scatter | solution.py:32
  240.0 17.0 %copy-start.5 = (bf16[1024,6144]{1,0:T(8,128)(2,1)S(1)}, bf16[1024,6144]{1,0:T(8,128)(2,1)}, u32[]{:S(2)}) copy-start(bf16[1024,6144]{1,0:T(8,128)(2,1)} %all-gather.4.cloned.1.call-done) | copy-start | bytes 37748740
  273.5 17.7 %copy-start.6 = (bf16[1024,768]{1,0:T(8,128)(2,1)S(1)}, bf16[1024,768]{1,0:T(8,128)(2,1)}, u32[]{:S(2)}) copy-start(bf16[1024,768]{1,0:T(8,128)(2,1)} %multiply_convert_fusion.1) | copy-start | bytes 4718596
Sparse Core Ops, SparseCore 0:
  9.6 13.6 reduce-scatter.2
  24.9 34.9 all-gather.5
  62.3 177.5 all-gather.3
  241.5 32.0 all-gather.7
  312.1 208.5 reduce-scatter.4

commit v2 on v1

v2 whole, which is shorter than its diff:
```python
import functools

import jax
import jax.numpy as jnp
from jax import lax
from jax.experimental import pallas as pl
from jax.experimental.pallas import tpu as pltpu
from jax.sharding import PartitionSpec as P

MESH = pl.DeviceIdType.MESH
CHUNKS = 6
TILE = 256
SLOTS = 3


def kernel(
    ring, columns, att, res, gain, gates, up, down, out, xs,
    up_v, down_v, att_in, hidden, x0, xv, act, rs_in, rs_out, g_in, g_col,
    ag_send, ag_recv, g_send, g_recv, rs_send, rs_recv, w_send, w_recv, att_sem, local_sem,
):
    f32, bf16 = jnp.float32, jnp.bfloat16
    rows, width = res.shape
    half = rows // 2
    chunk = width // CHUNKS
    split = up_v.shape[0]
    up_tiles = up_v.shape[2] // TILE
    deep = down_v.shape[1]
    line = ring // columns

    node = lax.axis_index("node")
    core = lax.axis_index("local")
    sibling = {"local": 1 - core}

    def node_at(place):
        if columns == 1:
            return place
        second = lax.div(place, line)
        return (place * (1 - second) + (ring - 1 - place) * second) * 2 + second

    if columns == 1:
        place = node
    else:
        z, y = lax.div(node, 2), lax.rem(node, 2)
        place = z * (1 - y) + (ring - 1 - z) * y
    ahead = ({"node": node_at(lax.rem(place + 1, ring))}, {"node": node_at(lax.rem(place + ring - 1, ring))})

    def part(h):
        return pl.ds(h * half, half)

    def remote(src, dst, send, recv, to):
        return pltpu.make_async_remote_copy(
            src_ref=src, dst_ref=dst, send_sem=send, recv_sem=recv, device_id=to, device_id_type=MESH
        )

    def rows_copy(h, s, src=None):
        src = xs.at[s, part(h)] if src is None else src
        return remote(src, xs.at[s + 1, part(h)], ag_send.at[h, s], ag_recv.at[h, s + 1], ahead[h])

    def gate_copy(h, s):
        return remote(g_in.at[h, s], g_in.at[h, s + 1], g_send.at[h, s], g_recv.at[h, s + 1], ahead[h])

    def sum_copy(h, c, s):
        now, then = lax.rem(s, 2), lax.rem(s + 1, SLOTS)
        return remote(
            rs_out.at[now, c, part(h)], rs_in.at[then, c, part(h)],
            rs_send.at[h, c, now], rs_recv.at[h, c, then], ahead[h],
        )

    barrier = pltpu.get_barrier_semaphore()
    for other in (sibling,) + ahead:
        pl.semaphore_signal(barrier, inc=1, device_id=other, device_id_type=MESH)
    pl.semaphore_wait(barrier, 3)

    att_copy = remote(
        att.at[0, pl.ds((1 - core) * rows, rows)], att_in, att_sem.at[0], att_sem.at[1], sibling
    )
    att_copy.start()
    own_att = pltpu.make_async_copy(att.at[0, pl.ds(core * rows, rows)], xv, local_sem.at[0])
    own_att.start()
    own_up = pltpu.make_async_copy(up.at[0], up_v.at[core], local_sem.at[1])
    own_down = pltpu.make_async_copy(down.at[0], down_v.at[core], local_sem.at[2])
    g_in[0, 0] = gates[...]
    g_in[1, 0] = gates[...]
    own_att.wait()
    att_copy.wait()
    up_copy = remote(up.at[0], up_v.at[core], w_send.at[0], w_recv.at[0], sibling)
    down_copy = remote(down.at[0], down_v.at[core], w_send.at[1], w_recv.at[1], sibling)
    up_copy.start()
    own_up.start()
    down_copy.start()
    own_down.start()

    for h in range(2):
        @pl.loop(0, half // 16)
        def _(i):
            at = pl.ds(pl.multiple_of(h * half + i * 16, 16), 16)
            state = res[at, :].astype(f32) + (xv[at, :].astype(f32) + att_in[at, :].astype(f32))
            hidden[at, :] = state
            mean_square = jnp.mean(state * state, axis=-1, keepdims=True)
            x0[at, :] = (state * lax.rsqrt(mean_square + 1e-06) * gain[...]).astype(bf16)

        gate_copy(h, 0).start()
        rows_copy(h, 0, x0.at[part(h)]).start()

    def take_gates(s):
        lane = lax.broadcasted_iota(jnp.int32, gates.shape, 1)
        expert = lax.broadcasted_iota(jnp.int32, gates.shape, 0)
        both = jnp.where(lane < half, g_in[0, s], g_in[1, s])
        row = jnp.sum(jnp.where(expert == node, both, 0.0), axis=0, keepdims=True)
        a = lax.broadcasted_iota(jnp.int32, (rows, rows), 0)
        b = lax.broadcasted_iota(jnp.int32, (rows, rows), 1)
        g_col[...] = jnp.sum(jnp.where(a == b, row, 0.0), axis=1, keepdims=True)

    def project_up(x):
        @pl.loop(0, split * up_tiles)
        def _(j):
            h, k = lax.div(j, up_tiles), lax.rem(j, up_tiles)
            v = jnp.dot(
                x[...], up_v[h, :, pl.ds(pl.multiple_of(k * TILE, TILE), TILE)],
                preferred_element_type=f32,
            )
            act[:, pl.ds(pl.multiple_of(j * TILE, TILE), TILE)] = (v / (1.0 + jnp.exp(-v))).astype(bf16)

    def project_down(at):
        total = jnp.dot(act[:, :deep], down_v[0, :, at], preferred_element_type=f32)
        for h in range(1, split):
            total = total + jnp.dot(
                act[:, h * deep:(h + 1) * deep], down_v[h, :, at], preferred_element_type=f32
            )
        return g_col[...] * total

    def arrive(s):
        for h in range(2):
            rows_copy(h, s - 1).wait_recv()
            gate_copy(h, s - 1).wait_recv()

            @pl.when(s < ring - 1)
            def _():
                gate_copy(h, s).start()
                rows_copy(h, s).start()

        load = pltpu.make_async_copy(xs.at[s], xv, local_sem.at[3])
        load.start()
        take_gates(s)
        load.wait()

    arrive(1)
    own_up.wait()
    up_copy.wait()
    project_up(xv)
    own_down.wait()
    down_copy.wait()

    def step(s, carry):
        now, slot = lax.rem(s, 2), lax.rem(s, SLOTS)

        def one(c, carry):
            @pl.when(s >= 2)
            def _():
                for h in range(2):
                    sum_copy(h, c, s - 1).wait_recv()

            @pl.when(s >= 3)
            def _():
                for h in range(2):
                    sum_copy(h, c, s - 2).wait_send()

            @pl.loop(0, chunk // TILE)
            def _(t):
                inner = pl.ds(pl.multiple_of(t * TILE, TILE), TILE)
                mine = project_down(pl.ds(pl.multiple_of(c * chunk + t * TILE, TILE), TILE))

                @pl.when(s >= 2)
                def _():
                    rs_out[now, c, :, inner] = (mine + rs_in[slot, c, :, inner].astype(f32)).astype(bf16)

                @pl.when(s < 2)
                def _():
                    rs_out[now, c, :, inner] = mine.astype(bf16)

            for h in range(2):
                sum_copy(h, c, s).start()
            return carry

        lax.fori_loop(0, CHUNKS, one, 0)

        @pl.when(s < ring - 1)
        def _():
            arrive(s + 1)
            project_up(xv)

        return carry

    lax.fori_loop(1, ring, step, 0)

    take_gates(0)
    project_up(x0)

    def last(c, carry):
        @pl.loop(0, chunk // TILE)
        def _(t):
            at = pl.ds(pl.multiple_of(c * chunk + t * TILE, TILE), TILE)
            hidden[:, at] = hidden[:, at] + project_down(at)

        return carry

    lax.fori_loop(0, CHUNKS, last, 0)

    def finish(c, carry):
        for h in range(2):
            sum_copy(h, c, jnp.int32(ring - 1)).wait_recv()

        @pl.loop(0, chunk // TILE)
        def _(t):
            inner = pl.ds(pl.multiple_of(t * TILE, TILE), TILE)
            at = pl.ds(pl.multiple_of(c * chunk + t * TILE, TILE), TILE)
            out[:, at] = (hidden[:, at] + rs_in[ring % SLOTS, c, :, inner].astype(f32)).astype(bf16)

        for h in range(2):
            sum_copy(h, c, jnp.int32(ring - 2)).wait_send()
            sum_copy(h, c, jnp.int32(ring - 1)).wait_send()
        return carry

    lax.fori_loop(0, CHUNKS, finish, 0)

    for h in range(2):
        rows_copy(h, 0, x0.at[part(h)]).wait_send()
        gate_copy(h, 0).wait_send()

    def drain(s, carry):
        for h in range(2):
            rows_copy(h, s).wait_send()
            gate_copy(h, s).wait_send()
        return carry

    lax.fori_loop(1, ring - 1, drain, 0)


def on_device(columns, attn_partial, residual, norm_gain, expert_ids, gate_weights, up_weight, down_weight):
    ring = lax.axis_size("node")
    split = lax.axis_size("local")
    rows, width = residual.shape
    part = up_weight.shape[2]
    bf16, f32 = jnp.bfloat16, jnp.float32
    experts = jnp.arange(ring, dtype=jnp.int32)
    gates = jnp.sum(
        jnp.where(expert_ids.T[:, None, :] == experts[None, :, None], gate_weights.T[:, None, :], 0.0),
        axis=0,
    )
    vmem = pl.BlockSpec(memory_space=pltpu.VMEM)
    anywhere = pl.BlockSpec(memory_space=pl.ANY)
    chunk = width // CHUNKS
    dma = pltpu.SemaphoreType.DMA
    layer_out, _ = pl.pallas_call(
        functools.partial(kernel, ring, columns),
        out_shape=(
            jax.ShapeDtypeStruct((rows, width), bf16),
            jax.ShapeDtypeStruct((ring, rows, width), bf16),
        ),
        in_specs=[anywhere, vmem, vmem, vmem, anywhere, anywhere],
        out_specs=(vmem, anywhere),
        scratch_shapes=[
            pltpu.VMEM((split, width, part), bf16),
            pltpu.VMEM((split, part, width), bf16),
            pltpu.VMEM((rows, width), bf16),
            pltpu.VMEM((rows, width), f32),
            pltpu.VMEM((rows, width), bf16),
            pltpu.VMEM((rows, width), bf16),
            pltpu.VMEM((rows, split * part), bf16),
            pltpu.VMEM((SLOTS, CHUNKS, rows, chunk), bf16),
            pltpu.VMEM((2, CHUNKS, rows, chunk), bf16),
            pltpu.VMEM((2, ring, ring, rows), f32),
            pltpu.VMEM((rows, 1), f32),
            dma((2, ring)),
            dma((2, ring)),
            dma((2, ring)),
            dma((2, ring)),
            dma((2, CHUNKS, 2)),
            dma((2, CHUNKS, SLOTS)),
            dma((2,)),
            dma((2,)),
            dma((2,)),
            dma((4,)),
        ],
        compiler_params=pltpu.CompilerParams(
            collective_id=0, has_side_effects=True, vmem_limit_bytes=62 * 1024 * 1024
        ),
        cost_estimate=pl.CostEstimate(
            flops=4 * ring * rows * width * part * split,
            bytes_accessed=2 * 2 * width * part,
            transcendentals=0,
        ),
    )(attn_partial, residual, norm_gain.reshape(1, width), gates, up_weight, down_weight)
    return layer_out


def solution(mesh):
    in_specs = (
        P("local", ("parts", "node"), None),
        P(("parts", "node", "local"), None),
        P(),
        P(("parts", "node", "local"), None),
        P(("parts", "node", "local"), None),
        P("node", None, "local"),
        P("node", "local", None),
    )
    out_specs = P(("parts", "node", "local"), None)
    columns = 2 if mesh.shape["parts"] == 2 else 1
    return jax.shard_map(
        functools.partial(on_device, columns), mesh=mesh, in_specs=in_specs, out_specs=out_specs,
        check_vma=False,
    )
```

time: 531 us -> 259 us (0.49)
  waiting for transfers between devices: 410 us -> 0 us
  Pallas kernels: 0 us -> 254 us
  matrix products: 69 us -> 0 us
  blocking collectives: 30.7 us -> 0 us
  between operations: 13.2 us -> 0.01 us
  other arithmetic: 7.21 us -> 1.3 us
    pallas_call x0 -> x1, Pallas kernels: none -> 254 us  [on_device(): pl.pallas_call(functools.partial(kernel, ring, columns), out_shape=(jax.S...]
    reduce_scatter x2 -> x0, waiting for transfers between devices: 224 us -> none  [the longest x1 209 us: on_device(): lax.psum_scatter(weighted, 'node', scatter_dimension=0, tiled=True)]
    all_gather x3 -> x0, waiting for transfers between devices: 184 us -> none  [the longest x1 180 us: on_device(): rows = lax.all_gather(normed, 'node', axis=0, tiled=True)]
    dot_general x4 -> x0, matrix products: 69 us -> none  [the longest x2 38.5 us: on_device(): jnp.dot(activated, down[half], preferred_element_type=jnp.float32)]
    all_gather x1 -> x0, blocking collectives: 30.7 us -> none  [on_device(): gates = lax.all_gather(dense_gates, 'node', axis=0, tiled=True)]
  transfers between devices with their start and end apart: 5 -> 0, of which waited for: 5 -> 0; matrix products, arithmetic and copies ran while one was open for 6% -> 0% of each run, Pallas kernels for 0% -> 0%
where the time goes in v2:
time: 259 us; the launch traced here: 258 us
  Pallas kernels  254 us (98%)
  local copies, waits for them, and re-layouts  2.69 us (1%)
    pallas_call x1, Pallas kernels, on_device(): pl.pallas_call(functools.partial(kernel, ring, columns), out_shape=(jax.S...  254 us

profile of v2, /device:TPU:0, one launch (start us, length us, event | category | flops | bytes accessed | tf_op | source)
XLA Modules:
  0.0 258.1 jit_solution(10909891632675108047)
XLA Ops:
  0.0 1.3 select_reduce_fusion.gates
  1.3 254.1 %shard_map.73 = (bf16[128,6144]{1,0:T(8,128)(2,1)}, bf16[8,128,6144]{2,1,0:T(8,128)(2,1)}) custom-call(bf16[1,256,6144]{2,1,0:T(8,128)(2,1)} %att.1, bf16[128,6144]{1,0:T(8,128)(2,1)} %res.1, f32[1,6144]{1,0:T(1,128)} %bitcast.5, f32[8,128]{1,0:T(8,128)} %select_reduce_fusion.gates, bf16[1,6144,768]{2,1,0:T(8,128)(2,1)} %up.1, bf16[1,768,6144]{2,1,0:T(8,128)(2,1)} %down.1), custom_call_target="tpu_custom_call" | custom-call | flops 38654705664 | bytes 18874368 | tf_op jit(solution)/shard_map/pallas_call | solution.py:254
  255.4 2.7 %copy.9 = bf16[128,6144]{1,0:T(8,128)(2,1)} copy(bf16[128,6144]{1,0:T(8,128)(2,1)} %get-tuple-element.6) | data formatting | bytes 3145728

commit v3 on v2

--- a/solution.py
+++ b/solution.py
@@ -11,12 +11,16 @@
 CHUNKS = 6
 TILE = 256
 SLOTS = 3
+LEAD = 2
+PASS_AT = 0
+PIECES = 2
 
 
 def kernel(
     ring, columns, att, res, gain, gates, up, down, out, xs,
     up_v, down_v, att_in, hidden, x0, xv, act, rs_in, rs_out, g_in, g_col,
-    ag_send, ag_recv, g_send, g_recv, rs_send, rs_recv, w_send, w_recv, att_sem, local_sem,
+    ag_send, ag_recv, g_send, g_recv, rs_send, rs_recv, w_send, w_recv,
+    att_send, att_recv, first_send, first_recv, local_sem,
 ):
     f32, bf16 = jnp.float32, jnp.bfloat16
     rows, width = res.shape
@@ -52,9 +56,8 @@
             src_ref=src, dst_ref=dst, send_sem=send, recv_sem=recv, device_id=to, device_id_type=MESH
         )
 
-    def rows_copy(h, s, src=None):
-        src = xs.at[s, part(h)] if src is None else src
-        return remote(src, xs.at[s + 1, part(h)], ag_send.at[h, s], ag_recv.at[h, s + 1], ahead[h])
+    def rows_copy(h, s):
+        return remote(xs.at[s, part(h)], xs.at[s + 1, part(h)], ag_send.at[h, s], ag_recv.at[h, s + 1], ahead[h])
 
     def gate_copy(h, s):
         return remote(g_in.at[h, s], g_in.at[h, s + 1], g_send.at[h, s], g_recv.at[h, s + 1], ahead[h])
@@ -71,36 +74,51 @@
         pl.semaphore_signal(barrier, inc=1, device_id=other, device_id_type=MESH)
     pl.semaphore_wait(barrier, 3)
 
-    att_copy = remote(
-        att.at[0, pl.ds((1 - core) * rows, rows)], att_in, att_sem.at[0], att_sem.at[1], sibling
-    )
-    att_copy.start()
+    piece = half // PIECES
+
+    def att_copy(h, q):
+        at = h * half + q * piece
+        return remote(
+            att.at[0, pl.ds((1 - core) * rows + at, piece)], att_in.at[pl.ds(at, piece)],
+            att_send.at[h, q], att_recv.at[h, q], sibling,
+        )
+
+    def first_copy(h, q):
+        at = pl.ds(h * half + q * piece, piece)
+        return remote(x0.at[at], xs.at[1, at], first_send.at[h, q], first_recv.at[h, q], ahead[h])
+
+    for q in range(PIECES):
+        for h in range(2):
+            att_copy(h, q).start()
     own_att = pltpu.make_async_copy(att.at[0, pl.ds(core * rows, rows)], xv, local_sem.at[0])
     own_att.start()
     own_up = pltpu.make_async_copy(up.at[0], up_v.at[core], local_sem.at[1])
     own_down = pltpu.make_async_copy(down.at[0], down_v.at[core], local_sem.at[2])
     g_in[0, 0] = gates[...]
     g_in[1, 0] = gates[...]
-    own_att.wait()
-    att_copy.wait()
     up_copy = remote(up.at[0], up_v.at[core], w_send.at[0], w_recv.at[0], sibling)
     down_copy = remote(down.at[0], down_v.at[core], w_send.at[1], w_recv.at[1], sibling)
-    up_copy.start()
-    own_up.start()
+    own_att.wait()
+    for q in range(PIECES):
+        for h in range(2):
+            att_copy(h, q).wait_recv()
+            if q == PIECES - 1 and h == 1:
+                up_copy.start()
+                own_up.start()
+
+            @pl.loop(0, piece // 16)
+            def _(i):
+                at = pl.ds(pl.multiple_of(h * half + q * piece + i * 16, 16), 16)
+                state = res[at, :].astype(f32) + (xv[at, :].astype(f32) + att_in[at, :].astype(f32))
+                hidden[at, :] = state
+                mean_square = jnp.mean(state * state, axis=-1, keepdims=True)
+                x0[at, :] = (state * lax.rsqrt(mean_square + 1e-06) * gain[...]).astype(bf16)
+
+            first_copy(h, q).start()
+            if q == 0:
+                gate_copy(h, 0).start()
     down_copy.start()
     own_down.start()
-
-    for h in range(2):
-        @pl.loop(0, half // 16)
-        def _(i):
-            at = pl.ds(pl.multiple_of(h * half + i * 16, 16), 16)
-            state = res[at, :].astype(f32) + (xv[at, :].astype(f32) + att_in[at, :].astype(f32))
-            hidden[at, :] = state
-            mean_square = jnp.mean(state * state, axis=-1, keepdims=True)
-            x0[at, :] = (state * lax.rsqrt(mean_square + 1e-06) * gain[...]).astype(bf16)
-
-        gate_copy(h, 0).start()
-        rows_copy(h, 0, x0.at[part(h)]).start()
 
     def take_gates(s):
         lane = lax.broadcasted_iota(jnp.int32, gates.shape, 1)
@@ -129,22 +147,29 @@
             )
         return g_col[...] * total
 
-    def arrive(s):
-        for h in range(2):
-            rows_copy(h, s - 1).wait_recv()
+    def pass_on(s):
+        for h in range(2):
             gate_copy(h, s - 1).wait_recv()
+            if isinstance(s, int) and s == 1:
+                for q in range(PIECES):
+                    first_copy(h, q).wait_recv()
+            else:
+                rows_copy(h, s - 1).wait_recv()
 
             @pl.when(s < ring - 1)
             def _():
                 gate_copy(h, s).start()
                 rows_copy(h, s).start()
 
-        load = pltpu.make_async_copy(xs.at[s], xv, local_sem.at[3])
-        load.start()
+    def load(s):
+        block = pltpu.make_async_copy(xs.at[s], xv, local_sem.at[3])
+        block.start()
         take_gates(s)
-        load.wait()
-
-    arrive(1)
+        block.wait()
+
+    for s in range(1, LEAD + 1):
+        pass_on(s)
+    load(1)
     own_up.wait()
     up_copy.wait()
     project_up(xv)
@@ -155,6 +180,10 @@
         now, slot = lax.rem(s, 2), lax.rem(s, SLOTS)
 
         def one(c, carry):
+            @pl.when((c == PASS_AT) & (s < ring - LEAD))
+            def _():
+                pass_on(s + LEAD)
+
             @pl.when(s >= 2)
             def _():
                 for h in range(2):
@@ -186,7 +215,7 @@
 
         @pl.when(s < ring - 1)
         def _():
-            arrive(s + 1)
+            load(s + 1)
             project_up(xv)
 
         return carry
@@ -224,7 +253,9 @@
     lax.fori_loop(0, CHUNKS, finish, 0)
 
     for h in range(2):
-        rows_copy(h, 0, x0.at[part(h)]).wait_send()
+        for q in range(PIECES):
+            att_copy(h, q).wait_send()
+            first_copy(h, q).wait_send()
         gate_copy(h, 0).wait_send()
 
     def drain(s, carry):
@@ -279,7 +310,10 @@
             dma((2, CHUNKS, SLOTS)),
             dma((2,)),
             dma((2,)),
-            dma((2,)),
+            dma((2, PIECES)),
+            dma((2, PIECES)),
+            dma((2, PIECES)),
+            dma((2, PIECES)),
             dma((4,)),
         ],
         compiler_params=pltpu.CompilerParams(

time: 259 us -> 259 us (level)
  no operation moved by 1% of the time
where the time goes in v3:
time: 259 us; the launch traced here: 258 us
  Pallas kernels  254 us (98%)
  local copies, waits for them, and re-layouts  2.69 us (1%)
    pallas_call x1, Pallas kernels, on_device(): pl.pallas_call(functools.partial(kernel, ring, columns), out_shape=(jax.S...  254 us

profile of v3, /device:TPU:0, one launch (start us, length us, event | category | flops | bytes accessed | tf_op | source)
XLA Modules:
  0.0 258.3 jit_solution(15503107868790330026)
XLA Ops:
  0.0 1.3 select_reduce_fusion.gates
  1.3 254.3 %shard_map.73 = (bf16[128,6144]{1,0:T(8,128)(2,1)}, bf16[8,128,6144]{2,1,0:T(8,128)(2,1)}) custom-call(bf16[1,256,6144]{2,1,0:T(8,128)(2,1)} %att.1, bf16[128,6144]{1,0:T(8,128)(2,1)} %res.1, f32[1,6144]{1,0:T(1,128)} %bitcast.5, f32[8,128]{1,0:T(8,128)} %select_reduce_fusion.gates, bf16[1,6144,768]{2,1,0:T(8,128)(2,1)} %up.1, bf16[1,768,6144]{2,1,0:T(8,128)(2,1)} %down.1), custom_call_target="tpu_custom_call" | custom-call | flops 38654705664 | bytes 18874368 | tf_op jit(solution)/shard_map/pallas_call | solution.py:285
  255.6 2.7 %copy.9 = bf16[128,6144]{1,0:T(8,128)(2,1)} copy(bf16[128,6144]{1,0:T(8,128)(2,1)} %get-tuple-element.6) | data formatting | bytes 3145728

commit v4 on v3

--- a/solution.py
+++ b/solution.py
@@ -11,7 +11,7 @@
 CHUNKS = 6
 TILE = 256
 SLOTS = 3
-LEAD = 2
+LEAD = 4
 PASS_AT = 0
 PIECES = 2
 

time: 259 us -> 260 us (level)
  no operation moved by 1% of the time
where the time goes in v4:
time: 260 us
  Pallas kernels  256 us (98%)
  local copies, waits for them, and re-layouts  2.69 us (1%)
    pallas_call x1, Pallas kernels, on_device(): pl.pallas_call(functools.partial(kernel, ring, columns), out_shape=(jax.S...  256 us

profile of v4, /device:TPU:0, one launch (start us, length us, event | category | flops | bytes accessed | tf_op | source)
XLA Modules:
  0.0 259.5 jit_solution(12768664764244149112)
XLA Ops:
  0.0 1.3 select_reduce_fusion.gates
  1.3 255.5 %shard_map.73 = (bf16[128,6144]{1,0:T(8,128)(2,1)}, bf16[8,128,6144]{2,1,0:T(8,128)(2,1)}) custom-call(bf16[1,256,6144]{2,1,0:T(8,128)(2,1)} %att.1, bf16[128,6144]{1,0:T(8,128)(2,1)} %res.1, f32[1,6144]{1,0:T(1,128)} %bitcast.5, f32[8,128]{1,0:T(8,128)} %select_reduce_fusion.gates, bf16[1,6144,768]{2,1,0:T(8,128)(2,1)} %up.1, bf16[1,768,6144]{2,1,0:T(8,128)(2,1)} %down.1), custom_call_target="tpu_custom_call" | custom-call | flops 38654705664 | bytes 18874368 | tf_op jit(solution)/shard_map/pallas_call | solution.py:285
  256.8 2.7 %copy.9 = bf16[128,6144]{1,0:T(8,128)(2,1)} copy(bf16[128,6144]{1,0:T(8,128)(2,1)} %get-tuple-element.6) | data formatting | bytes 3145728
